TPU v7x, 256 devices: a whole 4x4x8 slice. The times are simulated.
256 devices in a mesh: dp: 8 (over z), ctx: 32 (over x, y, core).
Axes of the slice: x: 4, y: 4, z: 8, core: 2. Of those that a mesh axis runs over, the one named last changes fastest.
Arguments:
- query_rows: bfloat16 [131072, 1024], P(('dp', 'ctx')), parts along dimension 0, may hold values from -6 to 6
- key_rows: bfloat16 [131072, 1024], P(('dp', 'ctx')), parts along dimension 0, may hold values from -6 to 6
- value_rows: bfloat16 [131072, 1024], P(('dp', 'ctx')), parts along dimension 0, may hold values from -6 to 6
- summary_pos: int32 [64, 16], P('dp'), parts along dimension 0, may hold values from 0 to 2047, as said below
Outputs:
- attended: bfloat16 [131072, 1024], P(('dp', 'ctx')), parts along dimension 0
There are 8 independent parts, one for each index of `dp`. A program takes and returns all parts, laid end to end along the dimension named above; each array names one. Nothing has to cross between parts.
Inputs may be any that keep to these rules, and one draw needn't show every extreme that they name: `summary_pos`: each row holds 16 distinct offsets.
All inputs are finite; a program needn't handle non-finite values.
Results may differ from a plain program's by a relative error of at most 0.003.
Values may be sent and summed in bfloat16 or wider, within the bound.
A program may use at most 192 MiB of HBM per device.

v0:
```python
import jax
import jax.numpy as jnp
from jax import lax
from jax.sharding import PartitionSpec as P

HD = 128
STRIDE = 2048


neg_floor = -1e30


def shifted(shard, axis, by):
    length = lax.axis_size(axis)
    pairs = [(i, i + by) for i in range(length) if 0 <= i + by < length]
    return lax.ppermute(shard, axis, pairs)


def head_columns(matrix, column, head_size):
    return lax.dynamic_slice_in_dim(matrix, column, head_size, 1)


def partial_softmax(query_head, key_head, value_head, allowed):
    score_scale = query_head.shape[1] ** (-0.5)
    scores = (
        lax.dot_general(
            query_head, key_head, (((1,), (1,)), ((), ())), preferred_element_type=jnp.float32
        )
        * score_scale
    )
    scores = jnp.where(allowed, scores, -jnp.inf)
    row_max = jnp.maximum(jnp.max(scores, axis=1), neg_floor)
    weights = jnp.exp(scores - row_max[:, None])
    weight_sum = jnp.sum(weights, axis=1)
    summed = jnp.dot(weights.astype(jnp.bfloat16), value_head, preferred_element_type=jnp.float32)
    return (summed, weight_sum, row_max)


def merge_partials(partials):
    row_max = partials[0][2]
    for partial_value in partials[1:]:
        row_max = jnp.maximum(row_max, partial_value[2])
    numerator = jnp.zeros_like(partials[0][0])
    denominator = jnp.zeros_like(row_max)
    for summed, weight_sum, group_max in partials:
        factor = jnp.exp(group_max - row_max)
        numerator = numerator + factor[:, None] * summed
        denominator = denominator + factor * weight_sum
    return (numerator / denominator[:, None]).astype(jnp.bfloat16)


def on_device(query_rows, key_rows, value_rows, summary_pos):
    tok_rows = query_rows.shape[0]
    feature_width = query_rows.shape[1]
    head_size = HD
    head_count = feature_width // head_size
    summary_count = summary_pos.shape[1]
    devices = lax.axis_size("ctx")
    shard_count = STRIDE // tok_rows
    device_index = lax.axis_index("ctx")
    shard_place = device_index % shard_count
    stride_index = device_index // shard_count
    key_value = jnp.stack([key_rows, value_rows])
    offsets = (
        lax.dynamic_index_in_dim(summary_pos, stride_index, 0, keepdims=False)
        - shard_place * tok_rows
    )
    owned_here = (offsets >= 0) & (offsets < tok_rows)
    picked = jnp.take(key_value, jnp.clip(offsets, 0, tok_rows - 1), axis=1)
    own_summary = jnp.where(owned_here[None, :, None], picked, jnp.zeros((), jnp.bfloat16))
    gathered = lax.all_gather(own_summary, "ctx", axis=1, tiled=True)
    source = jnp.arange(devices, dtype=jnp.int32)
    slot_offsets = jnp.repeat(summary_pos, shard_count, axis=0)
    owned = slot_offsets // tok_rows == (source % shard_count)[:, None]
    earlier = (source // shard_count < stride_index)[:, None]
    visible = (owned & earlier).reshape(1, devices * summary_count)
    remote_pairs = []
    for distance in range(1, shard_count):
        remote_pairs.append(shifted(key_value, "ctx", distance))
    block_rows = min(512, tok_rows)
    causal = (
        jnp.arange(block_rows, dtype=jnp.int32)[None, :]
        <= (jnp.arange(block_rows, dtype=jnp.int32) + 0)[:, None]
    )

    def one_head(head_index):
        column = head_index * head_size
        query_head = head_columns(query_rows, column, head_size)
        partials = [
            partial_softmax(
                query_head,
                head_columns(gathered[0], column, head_size),
                head_columns(gathered[1], column, head_size),
                visible,
            ),
            partial_softmax(
                query_head,
                head_columns(key_rows, column, head_size),
                head_columns(value_rows, column, head_size),
                causal,
            ),
        ]
        for distance in range(1, shard_count):
            usable = distance <= shard_place
            remote_pair = remote_pairs[distance - 1]
            partials.append(
                partial_softmax(
                    query_head,
                    head_columns(remote_pair[0], column, head_size),
                    head_columns(remote_pair[1], column, head_size),
                    usable,
                )
            )
        return merge_partials(partials)

    per_head = lax.map(one_head, jnp.arange(head_count, dtype=jnp.int32))
    outputs = jnp.transpose(per_head, (1, 0, 2)).reshape(block_rows, feature_width)
    return outputs


def solution(mesh):
    in_specs = (
        P(("dp", "ctx"), None),
        P(("dp", "ctx"), None),
        P(("dp", "ctx"), None),
        P("dp", None),
    )
    out_specs = P(("dp", "ctx"), None)
    return jax.shard_map(
        on_device, mesh=mesh, in_specs=in_specs, out_specs=out_specs, check_vma=False
    )
```

profile of v0, /device:TPU:1, one launch (start us, length us, event | category | flops | bytes accessed | tf_op | source)
XLA Modules:
  0.0 353.3 jit_solution(14400919333195490889)
XLA Ops:
  7.4 2.8 copy.18
  11.8 5.6 %pad_maximum_fusion = bf16[2,512,1024]{2,0,1:T(2,128)(2,1)} fusion(bf16[1,512,1024]{2,0,1:T(2,128)(2,1)S(1)} %copy.19, bf16[1,512,1024]{2,0,1:T(2,128)(2,1)S(1)} %copy.18), kind=kLoop, calls=%fused_computation.97 | loop fusion | flops 4194304 | bytes 4194304 | tf_op jit(solution)/shard_map/stack | solution.py:63
  17.5 2.3 gather_fusion
  20.6 4.6 %collective-permute-start = (bf16[2,512,1024]{2,0,1:T(2,128)(2,1)}, bf16[2,512,1024]{2,0,1:T(2,128)(2,1)}, u32[]{:S(2)}, u32[]{:S(2)}) collective-permute-start(bf16[2,512,1024]{2,0,1:T(2,128)(2,1)} %pad_maximum_fusion), channel_id=1, source_target_pairs={{0,1},{1,2},{2,3},{3,4},{4,5},{5,6},{6,7},{7,8},{8,9},{9,10},{10,1... | collective-permute-start | bytes 6291464 | tf_op jit(solution)/shard_map/ppermute | solution.py:16
  25.2 4.6 %collective-permute-start.1 = (bf16[2,512,1024]{2,0,1:T(2,128)(2,1)}, bf16[2,512,1024]{2,0,1:T(2,128)(2,1)}, u32[]{:S(2)}, u32[]{:S(2)}) collective-permute-start(bf16[2,512,1024]{2,0,1:T(2,128)(2,1)} %pad_maximum_fusion), channel_id=1, source_target_pairs={{0,2},{1,3},{2,4},{3,5},{4,6},{5,7},{6,8},{7,9},{8,10},{9,11},{10,... | collective-permute-start | bytes 6291464 | tf_op jit(solution)/shard_map/ppermute | solution.py:16
  29.8 3.5 collective-permute-start.2
  33.3 35.7 %collective-permute-done = bf16[2,512,1024]{2,0,1:T(2,128)(2,1)} collective-permute-done((bf16[2,512,1024]{2,0,1:T(2,128)(2,1)}, bf16[2,512,1024]{2,0,1:T(2,128)(2,1)}, u32[]{:S(2)}, u32[]{:S(2)}) %collective-permute-start) | collective-permute-done | bytes 2097184 | tf_op jit(solution)/shard_map/ppermute | solution.py:16
  69.0 2.2 copy.21
  71.2 42.7 %collective-permute-done.1 = bf16[2,512,1024]{2,0,1:T(2,128)(2,1)} collective-permute-done((bf16[2,512,1024]{2,0,1:T(2,128)(2,1)}, bf16[2,512,1024]{2,0,1:T(2,128)(2,1)}, u32[]{:S(2)}, u32[]{:S(2)}) %collective-permute-start.1) | collective-permute-done | bytes 2097184 | tf_op jit(solution)/shard_map/ppermute | solution.py:16
  113.9 3.6 %copy.22 = bf16[2,512,1024]{2,1,0:T(8,128)(2,1)} copy(bf16[2,512,1024]{2,0,1:T(2,128)(2,1)} %collective-permute-done.1) | data formatting | bytes 4194304
  117.5 21.8 %collective-permute-done.2 = bf16[2,512,1024]{2,0,1:T(2,128)(2,1)} collective-permute-done((bf16[2,512,1024]{2,0,1:T(2,128)(2,1)}, bf16[2,512,1024]{2,0,1:T(2,128)(2,1)}, u32[]{:S(2)}, u32[]{:S(2)}) %collective-permute-start.2) | collective-permute-done | bytes 2097184 | tf_op jit(solution)/shard_map/ppermute | solution.py:16
  139.3 3.5 copy.23
  142.8 47.6 %all-gather.2.cloned.1.call-done = bf16[2,512,1024]{2,0,1:T(2,128)(2,1)} async-done(((bf16[2,16,1024]{2,0,1:T(2,128)(2,1)}), bf16[2,512,1024]{2,0,1:T(2,128)(2,1)}) %all-gather.2.cloned.1.call-update) | async-done | bytes 2097168 | tf_op jit(solution)/shard_map/all_gather | solution.py:71
  190.4 3.5 %copy.20 = bf16[2,512,1024]{2,1,0:T(8,128)(2,1)} copy(bf16[2,512,1024]{2,0,1:T(2,128)(2,1)} %all-gather.2.cloned.1.call-done) | data formatting | bytes 4194304
  193.9 150.2 %while.13 = (s32[]{:T(128)}, bf16[8,512,128]{2,1,0:T(8,128)(2,1)}, s32[8]{0:T(128)S(1)}, bf16[512,1024]{1,0:T(8,128)(2,1)}, bf16[2,512,1024]{2,1,0:T(8,128)(2,1)...) while((s32[]{:T(128)}, bf16[8,512,128]{2,1,0:T(8,128)(2,1)}, ...), condition=%wide.region_11.12_spmd.clone, body=%wide.region_0.11_spmd.clone.sunk | while | flops 681264640 | bytes 45226940 | solution.py:116
  195.1 3.3 fusion.120
  213.9 3.3 fusion.120
  232.7 3.3 fusion.120
  251.5 3.3 fusion.120
  270.3 3.3 fusion.120
  289.1 3.3 fusion.120
  307.9 3.3 fusion.120
  326.6 3.3 fusion.120
  344.1 2.4 copy_bitcast_fusion
  (240 shorter events, 121.4 us)
Async XLA Ops:
  6.5 3.7 %copy-start.1 = (bf16[512,1024]{1,0:T(8,128)(2,1)S(1)}, bf16[512,1024]{1,0:T(8,128)(2,1)}, u32[]{:S(2)}) copy-start(bf16[512,1024]{1,0:T(8,128)(2,1)} %param.8) | copy-start | bytes 3145732
  6.5 183.8 %all-gather.2.cloned.1.call-start = ((), (), s32[]{:S(2)}) async-start(), calls=%async_computation | async-start | bytes 2162688 | tf_op jit(solution)/shard_map/all_gather | solution.py:71
  20.6 48.4 %collective-permute-start = (bf16[2,512,1024]{2,0,1:T(2,128)(2,1)}, bf16[2,512,1024]{2,0,1:T(2,128)(2,1)}, u32[]{:S(2)}, u32[]{:S(2)}) collective-permute-start(bf16[2,512,1024]{2,0,1:T(2,128)(2,1)} %pad_maximum_fusion), channel_id=1, source_target_pairs={{0,1},{1,2},{2,3},{3,4},{4,5},{5,6},{6,7},{7,8},{8,9},{9,10},{10,1... | collective-permute-start | bytes 6291464 | tf_op jit(solution)/shard_map/ppermute | solution.py:16
  25.2 88.7 %collective-permute-start.1 = (bf16[2,512,1024]{2,0,1:T(2,128)(2,1)}, bf16[2,512,1024]{2,0,1:T(2,128)(2,1)}, u32[]{:S(2)}, u32[]{:S(2)}) collective-permute-start(bf16[2,512,1024]{2,0,1:T(2,128)(2,1)} %pad_maximum_fusion), channel_id=1, source_target_pairs={{0,2},{1,3},{2,4},{3,5},{4,6},{5,7},{6,8},{7,9},{8,10},{9,11},{10,... | collective-permute-start | bytes 6291464 | tf_op jit(solution)/shard_map/ppermute | solution.py:16
  29.8 109.5 %collective-permute-start.2 = (bf16[2,512,1024]{2,0,1:T(2,128)(2,1)}, bf16[2,512,1024]{2,0,1:T(2,128)(2,1)}, u32[]{:S(2)}, u32[]{:S(2)}) collective-permute-start(bf16[2,512,1024]{2,0,1:T(2,128)(2,1)} %pad_maximum_fusion), channel_id=1, source_target_pairs={{0,3},{1,4},{2,5},{3,6},{4,7},{5,8},{6,9},{7,10},{8,11},{9,12},{10... | collective-permute-start | bytes 6291464 | tf_op jit(solution)/shard_map/ppermute | solution.py:16
  142.8 51.1 %copy-start.2 = (s32[8,16]{1,0:T(8,128)S(1)}, s32[8,16]{1,0:T(8,128)}, u32[]{:S(2)}) copy-start(s32[8,16]{1,0:T(8,128)} %param.9) | copy-start | bytes 1540
  198.8 2.8 copy-start
  217.6 2.8 copy-start
  236.4 2.8 copy-start
  255.2 2.8 copy-start
  274.0 2.8 copy-start
  292.8 2.8 copy-start
  311.6 2.8 copy-start
  330.3 2.8 copy-start
Sparse Core Ops, SparseCore 0:
  20.7 169.6 all-gather.1
where the time goes:
time: 355 us; the launch traced here: 353 us
  waiting for transfers between devices  148 us (42%)
  matrix products  86 us (24%)
  local copies, waits for them, and re-layouts  71.9 us (20%)
  other arithmetic  15.6 us (4%)
  between operations  13.5 us (4%)
  starting transfers between devices  12.7 us (4%)
  loops' own time  5.85 us (2%)
    ppermute x3, waiting for transfers between devices, shifted(): return lax.ppermute(shard, axis, pairs)  100 us
    dot_general x40, matrix products, partial_softmax(): lax.dot_general(query_head, key_head, (((1,), (1,)), ((), ())), preferred...  51.7 us
    all_gather x1, waiting for transfers between devices, on_device(): gathered = lax.all_gather(own_summary, 'ctx', axis=1, tiled=True)  47.6 us
    slice x16, local copies, waits for them, and re-layouts, one_head(): remote_pair[1]  42.1 us
    dot_general x40, matrix products, partial_softmax(): jnp.dot(weights.astype(jnp.bfloat16), value_head, preferred_element_type=...  34.4 us
    unnamed x8, local copies, waits for them, and re-layouts  12.8 us
    ppermute x3, starting transfers between devices, shifted(): return lax.ppermute(shard, axis, pairs)  12.7 us
    reduce_sum x40, other arithmetic, partial_softmax(): weight_sum = jnp.sum(weights, axis=1)  7.83 us
  transfers between devices with their start and end apart: 4, of which 4 were waited for; matrix products, arithmetic and copies ran while one was open for 3% of the time, Pallas kernels for 0%

commit v1 on v0

v1 whole, which is shorter than its diff:
```python
import functools

import jax
import jax.numpy as jnp
import numpy as np
from jax import lax
from jax.experimental import pallas as pl
from jax.experimental.pallas import tpu as pltpu
from jax.sharding import PartitionSpec as P

MESH = pl.DeviceIdType.MESH
HEADS = 8
HD = 128
ROWS = 512
SUMS = 16
STRIDES = 8
X = 4
RATE = float(HD**-0.5 * np.log2(np.e))
FLOOR = -1.0e30


def scores(keys, queries):
    return lax.dot_general(
        keys, queries, (((1,), (1,)), ((), ())), preferred_element_type=jnp.float32
    )


def attend(parts, queries):
    raw = []
    for keys, _, mask in parts:
        s = scores(keys, queries)
        raw.append(s if mask is None else jnp.where(mask, s, FLOOR))
    top = functools.reduce(jnp.maximum, [jnp.max(s, axis=0, keepdims=True) for s in raw]) * RATE
    total = None
    weight = None
    for s, (_, values, _) in zip(raw, parts):
        p = jnp.exp2(s * RATE - top)
        part_weight = jnp.sum(p, axis=0, keepdims=True)
        part = jnp.dot(values, p.astype(jnp.bfloat16), preferred_element_type=jnp.float32)
        total = part if total is None else total + part
        weight = part_weight if weight is None else weight + part_weight
    return total, top, weight


def kernel(
    q_hbm, k_hbm, v_hbm, pos_ref, out_hbm,
    q, k, v, kx, vt, vtx, qr, o_send, o_recv, lse_send, lse_recv,
    acc, acc_max, acc_sum, staged, own_rows, half_recv, half, pair_recv, table,
    load_sem, q_s, q_r, kx_s, kx_r, vt_s, vt_r, o_s, o_r, l_s, l_r, out_sem, st_s, st_r, x_s, x_r,
):
    me = lax.axis_index("ctx")
    core = me % 2
    y = (me // 2) % 4
    x = me // 8
    first = y % 2 == 0
    place = me % 4
    group = y // 2
    stride = x * 2 + group
    peer = me + 1 - 2 * core
    partner = jnp.where(first, me + 2, me - 2)
    beside = x * 8 + (jnp.where(first, y + 3, y + 1) % 4) * 2 + core
    along = [((x + d) % X) * 8 + y * 2 + core for d in range(1, X)]

    loads = [
        pltpu.make_async_copy(src, dst, load_sem.at[n])
        for n, (src, dst) in enumerate(((k_hbm, k), (v_hbm, v), (q_hbm, q)))
    ]
    for load in loads:
        load.start()

    barrier = pltpu.get_barrier_semaphore()
    for other in (peer, partner, beside, *along):
        pl.semaphore_signal(barrier, inc=1, device_id={"ctx": other}, device_id_type=MESH)
    pl.semaphore_wait(barrier, 6)

    def cols(h):
        return pl.ds(pl.multiple_of(h * HD, HD), HD)

    def remote(src, dst, s, r, to):
        return pltpu.make_async_remote_copy(
            src_ref=src, dst_ref=dst, send_sem=s, recv_sem=r, device_id={"ctx": to}, device_id_type=MESH
        )

    def q_copy(h):
        return remote(q_hbm.at[:, cols(h)], qr.at[h], q_s.at[h], q_r.at[h], partner)

    def o_copy(h):
        return remote(o_send.at[h], o_recv.at[h], o_s.at[h], o_r.at[h], partner)

    def lse_copy(h):
        return remote(lse_send.at[h], lse_recv.at[h], l_s.at[h], l_r.at[h], partner)

    def vt_copy(h):
        return remote(vt.at[h], vtx.at[h], vt_s.at[h], vt_r.at[h], peer)

    kx_copy = remote(k_hbm, kx, kx_s, kx_r, peer)
    gives = place != 3
    takes = place != 2
    half_copy = remote(own_rows.at[1 - core], half_recv, st_s.at[0], st_r.at[0], peer)
    pair_copy = remote(half, pair_recv, st_s.at[1], st_r.at[1], partner)
    slot = table.at[core, :, pl.ds(pl.multiple_of((group * X + x) * SUMS, SUMS), SUMS), :]
    x_copies = [remote(slot, slot, x_s.at[n], x_r.at[n], to) for n, to in enumerate(along)]
    side = table.at[core, :, pl.ds(pl.multiple_of(group * X * SUMS, X * SUMS), X * SUMS), :]
    side_copy = remote(side, side, st_s.at[2], st_r.at[2], beside)
    table_copy = remote(table.at[core], table.at[core], st_s.at[3], st_r.at[3], peer)

    @pl.when(jnp.logical_not(first))
    def _():
        def send(h, _):
            q_copy(h).start()
            return 0

        lax.fori_loop(0, HEADS, send, 0)

    @pl.when(gives)
    def _():
        kx_copy.start()

    loads[0].wait()
    loads[1].wait()

    def turn(h, _):
        vt[h] = v[:, cols(h)].T

        @pl.when(gives)
        def _():
            vt_copy(h).start()

        return 0

    lax.fori_loop(0, HEADS, turn, 0)

    offset = lax.broadcasted_iota(jnp.int32, (SUMS, ROWS), 1) + place * ROWS
    row = lax.broadcasted_iota(jnp.int32, (SUMS, ROWS), 0)
    wanted = jnp.zeros((SUMS, ROWS), jnp.int32)
    for c in range(SUMS):
        wanted = jnp.where(row == c, pos_ref[stride, c], wanted)
    pick = jnp.where(offset == wanted, 1.0, 0.0).astype(jnp.bfloat16)

    def pick_rows(h, _):
        own_rows[0, h] = jnp.dot(pick, k[:, cols(h)], preferred_element_type=jnp.float32).astype(jnp.bfloat16)
        own_rows[1, h] = jnp.dot(pick, v[:, cols(h)], preferred_element_type=jnp.float32).astype(jnp.bfloat16)
        return 0

    lax.fori_loop(0, HEADS, pick_rows, 0)
    half_copy.start()
    loads[2].wait()

    key_id = lax.broadcasted_iota(jnp.int32, (ROWS, ROWS), 0)
    query_id = lax.broadcasted_iota(jnp.int32, (ROWS, ROWS), 1)

    def local(h):
        def keep(parts):
            total, top, weight = attend(parts, q[:, cols(h)])
            acc[h] = total
            acc_max[h] = top
            acc_sum[h] = weight

        @pl.when(core == 0)
        def _():
            keep([(k[:, cols(h)], vt[h], key_id <= query_id)])

        @pl.when(core == 1)
        def _():
            keep([(k[:, cols(h)], vt[h], key_id <= query_id), (kx[:, cols(h)], vtx[h], None)])

    def finish(h, remote_part):
        seen = lax.broadcasted_iota(jnp.int32, (STRIDES * SUMS, ROWS), 0) // SUMS
        seen = (seen % X) * 2 + seen // X < stride
        total, top, weight = attend([(table[0, h], table[1, h].T, seen)], q[:, cols(h)])
        high = jnp.maximum(top, acc_max[h])
        if remote_part:
            high = jnp.maximum(high, lse_recv[h])
        scale_sum = jnp.exp2(top - high)
        scale_own = jnp.exp2(acc_max[h] - high)
        top_part = total * scale_sum + acc[h] * scale_own
        low_part = weight * scale_sum + acc_sum[h] * scale_own
        if remote_part:
            scale_far = jnp.exp2(lse_recv[h] - high)
            top_part = top_part + o_recv[h].astype(jnp.float32) * scale_far
            low_part = low_part + scale_far
        staged[h] = (top_part / low_part).astype(jnp.bfloat16).T
        out_copy(h).start()

    def out_copy(h):
        return pltpu.make_async_copy(staged.at[h], out_hbm.at[:, cols(h)], out_sem.at[h])

    def stage_pair():
        half_copy.wait_recv()
        half[...] = own_rows[core] + half_recv[...]
        pair_copy.start()

    def stage_x():
        pair_copy.wait_recv()
        table[core, :, pl.ds(pl.multiple_of((group * X + x) * SUMS, SUMS), SUMS), :] = half[...] + pair_recv[...]
        for copy in x_copies:
            copy.start()

    def stage_side():
        for copy in x_copies:
            copy.wait_recv()
        side_copy.start()

    def stage_table():
        side_copy.wait_recv()
        table_copy.start()

    def step(h, _):
        @pl.when((h == 0) & takes)
        def _():
            kx_copy.wait_recv()

        @pl.when(takes)
        def _():
            vt_copy(h).wait_recv()

        local(h)
        pl.when(h == 0)(stage_pair)
        pl.when(h == 1)(stage_side)

        @pl.when(first)
        def _():
            q_copy(h).wait_recv()
            total, top, weight = attend(
                [(k[:, cols(h)], vt[h], None), (kx[:, cols(h)], vtx[h], None)], qr[h]
            )
            o_send[h] = (total / weight).astype(jnp.bfloat16)
            lse_send[h] = top + jnp.log2(weight)
            o_copy(h).start()
            lse_copy(h).start()

        pl.when(h == 0)(stage_x)
        pl.when(h == 1)(stage_table)

        @pl.when(h == 3)
        def _():
            table_copy.wait_recv()

        @pl.when(first & (h >= 4))
        def _():
            finish(2 * (h - 4), False)
            finish(2 * (h - 4) + 1, False)

        return 0

    lax.fori_loop(0, HEADS, step, 0)

    @pl.when(jnp.logical_not(first))
    def _():
        def merge(h, _):
            o_copy(h).wait_recv()
            lse_copy(h).wait_recv()
            finish(h, True)
            return 0

        lax.fori_loop(0, HEADS, merge, 0)

    def drain(h, _):
        out_copy(h).wait()

        @pl.when(gives)
        def _():
            vt_copy(h).wait_send()

        @pl.when(first)
        def _():
            o_copy(h).wait_send()
            lse_copy(h).wait_send()

        @pl.when(jnp.logical_not(first))
        def _():
            q_copy(h).wait_send()

        return 0

    lax.fori_loop(0, HEADS, drain, 0)

    @pl.when(gives)
    def _():
        kx_copy.wait_send()

    for copy in (half_copy, pair_copy, *x_copies, side_copy, table_copy):
        copy.wait_send()


def on_device(query_rows, key_rows, value_rows, summary_pos):
    bf16, f32 = jnp.bfloat16, jnp.float32
    dma = pltpu.SemaphoreType.DMA
    anywhere = pl.BlockSpec(memory_space=pl.ANY)
    per_head = dma((HEADS,))
    return pl.pallas_call(
        kernel,
        out_shape=jax.ShapeDtypeStruct(query_rows.shape, bf16),
        in_specs=[anywhere] * 3 + [pl.BlockSpec(memory_space=pltpu.SMEM)],
        out_specs=anywhere,
        scratch_shapes=[
            pltpu.VMEM((ROWS, HEADS * HD), bf16),
            pltpu.VMEM((ROWS, HEADS * HD), bf16),
            pltpu.VMEM((ROWS, HEADS * HD), bf16),
            pltpu.VMEM((ROWS, HEADS * HD), bf16),
            pltpu.VMEM((HEADS, HD, ROWS), bf16),
            pltpu.VMEM((HEADS, HD, ROWS), bf16),
            pltpu.VMEM((HEADS, ROWS, HD), bf16),
            pltpu.VMEM((HEADS, HD, ROWS), bf16),
            pltpu.VMEM((HEADS, HD, ROWS), bf16),
            pltpu.VMEM((HEADS, 1, ROWS), f32),
            pltpu.VMEM((HEADS, 1, ROWS), f32),
            pltpu.VMEM((HEADS, HD, ROWS), f32),
            pltpu.VMEM((HEADS, 1, ROWS), f32),
            pltpu.VMEM((HEADS, 1, ROWS), f32),
            pltpu.VMEM((HEADS, ROWS, HD), bf16),
            pltpu.VMEM((2, HEADS, SUMS, HD), bf16),
            pltpu.VMEM((HEADS, SUMS, HD), bf16),
            pltpu.VMEM((HEADS, SUMS, HD), bf16),
            pltpu.VMEM((HEADS, SUMS, HD), bf16),
            pltpu.VMEM((2, HEADS, STRIDES * SUMS, HD), bf16),
            dma((3,)),
            per_head, per_head,
            dma, dma,
            per_head, per_head,
            per_head, per_head,
            per_head, per_head,
            per_head,
            dma((4,)), dma((4,)),
            dma((X - 1,)), dma((X - 1,)),
        ],
        compiler_params=pltpu.CompilerParams(
            collective_id=0, has_side_effects=True, vmem_limit_bytes=56 * 2**20
        ),
    )(query_rows, key_rows, value_rows, summary_pos)


def solution(mesh):
    tokens = P(("dp", "ctx"), None)
    return jax.shard_map(
        on_device,
        mesh=mesh,
        in_specs=(tokens, tokens, tokens, P("dp", None)),
        out_specs=tokens,
        check_vma=False,
    )
```

time: 355 us -> 58.5 us (0.16)
  the two profiles are of different devices: /device:TPU:1 before, /device:TPU:232 now
where the time goes in v1:
time: 58.5 us; the launch traced here: 58.3 us
  Pallas kernels  56.1 us (96%)
  local copies, waits for them, and re-layouts  2.26 us (4%)
    pallas_call x1, Pallas kernels, on_device(): pl.pallas_call(kernel, out_shape=jax.ShapeDtypeStruct(query_rows.shape, b...  56.1 us
    unnamed x1, local copies, waits for them, and re-layouts  2.26 us

profile of v1, /device:TPU:232, one launch (start us, length us, event | category | flops | bytes accessed | tf_op | source)
XLA Modules:
  0.0 58.3 jit_solution(11319190212196237210)
XLA Ops:
  0.0 56.1 %shard_map.46 = bf16[512,1024]{1,0:T(8,128)(2,1)} custom-call(bf16[512,1024]{1,0:T(8,128)(2,1)} %q_hbm.1, bf16[512,1024]{1,0:T(8,128)(2,1)} %k_hbm.1, bf16[512,1024]{1,0:T(8,128)(2,1)} %v_hbm.1, s32[8,16]{1,0:T(8,128)} %pos_ref.1), custom_call_target="tpu_custom_call" | custom-call | tf_op jit(solution)/shard_map/pallas_call | solution.py:291
  56.1 2.3 %copy.6 = bf16[512,1024]{1,0:T(8,128)(2,1)} copy(bf16[512,1024]{1,0:T(8,128)(2,1)} %shard_map.46) | data formatting | bytes 2097152

commit v2 on v1

--- a/solution.py
+++ b/solution.py
@@ -106,11 +106,7 @@
 
     @pl.when(jnp.logical_not(first))
     def _():
-        def send(h, _):
-            q_copy(h).start()
-            return 0
-
-        lax.fori_loop(0, HEADS, send, 0)
+        q_copy(0).start()
 
     @pl.when(gives)
     def _():
@@ -119,16 +115,10 @@
     loads[0].wait()
     loads[1].wait()
 
-    def turn(h, _):
-        vt[h] = v[:, cols(h)].T
-
-        @pl.when(gives)
-        def _():
-            vt_copy(h).start()
-
-        return 0
-
-    lax.fori_loop(0, HEADS, turn, 0)
+    def stage_pair():
+        half_copy.wait_recv()
+        half[...] = own_rows[core] + half_recv[...]
+        pair_copy.start()
 
     offset = lax.broadcasted_iota(jnp.int32, (SUMS, ROWS), 1) + place * ROWS
     row = lax.broadcasted_iota(jnp.int32, (SUMS, ROWS), 0)
@@ -137,13 +127,32 @@
         wanted = jnp.where(row == c, pos_ref[stride, c], wanted)
     pick = jnp.where(offset == wanted, 1.0, 0.0).astype(jnp.bfloat16)
 
-    def pick_rows(h, _):
-        own_rows[0, h] = jnp.dot(pick, k[:, cols(h)], preferred_element_type=jnp.float32).astype(jnp.bfloat16)
-        own_rows[1, h] = jnp.dot(pick, v[:, cols(h)], preferred_element_type=jnp.float32).astype(jnp.bfloat16)
+    for part, rows in enumerate((k, v)):
+        picked = jnp.dot(pick, rows[...], preferred_element_type=jnp.float32).astype(jnp.bfloat16)
+        for h in range(HEADS):
+            own_rows[part, h] = picked[:, h * HD : (h + 1) * HD]
+    half_copy.start()
+
+    def turn(h, _):
+        vt[h] = v[:, cols(h)].T
+
+        @pl.when(gives)
+        def _():
+            vt_copy(h).start()
+
         return 0
 
-    lax.fori_loop(0, HEADS, pick_rows, 0)
-    half_copy.start()
+    lax.fori_loop(0, HEADS, turn, 0)
+    stage_pair()
+
+    @pl.when(jnp.logical_not(first))
+    def _():
+        def send(h, _):
+            q_copy(h).start()
+            return 0
+
+        lax.fori_loop(1, HEADS, send, 0)
+
     loads[2].wait()
 
     key_id = lax.broadcasted_iota(jnp.int32, (ROWS, ROWS), 0)
@@ -185,11 +194,6 @@
     def out_copy(h):
         return pltpu.make_async_copy(staged.at[h], out_hbm.at[:, cols(h)], out_sem.at[h])
 
-    def stage_pair():
-        half_copy.wait_recv()
-        half[...] = own_rows[core] + half_recv[...]
-        pair_copy.start()
-
     def stage_x():
         pair_copy.wait_recv()
         table[core, :, pl.ds(pl.multiple_of((group * X + x) * SUMS, SUMS), SUMS), :] = half[...] + pair_recv[...]
@@ -215,7 +219,6 @@
             vt_copy(h).wait_recv()
 
         local(h)
-        pl.when(h == 0)(stage_pair)
         pl.when(h == 1)(stage_side)
 
         @pl.when(first)
@@ -325,9 +328,9 @@
             dma((X - 1,)), dma((X - 1,)),
         ],
         compiler_params=pltpu.CompilerParams(
-            collective_id=0, has_side_effects=True, vmem_limit_bytes=56 * 2**20
+            collective_id=0, has_side_effects=True, vmem_limit_bytes=52 * 2**20
         ),
-    )(query_rows, key_rows, value_rows, summary_pos)
+    )(*(pltpu.with_memory_space_constraint(a, pltpu.HBM) for a in (query_rows, key_rows, value_rows, summary_pos)))
 
 
 def solution(mesh):

time: 58.5 us -> 40.1 us (0.69)
  the two profiles are of different devices: /device:TPU:232 before, /device:TPU:206 now
where the time goes in v2:
time: 40.1 us; the launch traced here: 40 us
  Pallas kernels  39 us (97%)
  local copies, waits for them, and re-layouts  0.97 us (2%)
    pallas_call x1, Pallas kernels, on_device(): pl.pallas_call(kernel, out_shape=jax.ShapeDtypeStruct(query_rows.shape, b...  39 us
    unnamed x1, local copies, waits for them, and re-layouts  0.97 us

profile of v2, /device:TPU:206, one launch (start us, length us, event | category | flops | bytes accessed | tf_op | source)
XLA Modules:
  0.0 40.0 jit_solution(7842004943483688285)
XLA Ops:
  0.0 39.0 %shard_map.46 = bf16[512,1024]{1,0:T(8,128)(2,1)S(1)} custom-call(bf16[512,1024]{1,0:T(8,128)(2,1)} %q_hbm.1, bf16[512,1024]{1,0:T(8,128)(2,1)} %k_hbm.1, bf16[512,1024]{1,0:T(8,128)(2,1)} %v_hbm.1, s32[8,16]{1,0:T(8,128)} %pos_ref.1), custom_call_target="tpu_custom_call" | custom-call | tf_op jit(solution)/shard_map/pallas_call | solution.py:294
  39.0 1.0 %copy.6 = bf16[512,1024]{1,0:T(8,128)(2,1)} copy(bf16[512,1024]{1,0:T(8,128)(2,1)S(1)} %shard_map.46) | data formatting | bytes 2097152

commit v3 on v2

--- a/solution.py
+++ b/solution.py
@@ -17,6 +17,7 @@
 X = 4
 RATE = float(HD**-0.5 * np.log2(np.e))
 FLOOR = -1.0e30
+KEPT = HEADS - 1
 
 
 def scores(keys, queries):
@@ -45,20 +46,25 @@
 def kernel(
     q_hbm, k_hbm, v_hbm, pos_ref, out_hbm,
     q, k, v, kx, vt, vtx, qr, o_send, o_recv, lse_send, lse_recv,
-    acc, acc_max, acc_sum, staged, own_rows, half_recv, half, pair_recv, table,
-    load_sem, q_s, q_r, kx_s, kx_r, vt_s, vt_r, o_s, o_r, l_s, l_r, out_sem, st_s, st_r, x_s, x_r,
+    acc, acc_max, acc_sum, staged, own_rows, rows_recv, chip_rows, pair_recv, table, kf, vf,
+    load_sem, q_s, q_r, kx_s, kx_r, vt_s, vt_r, o_s, o_r, l_s, l_r, out_sem, st_s, st_r, x_s, x_r, f_s, f_r, ready,
 ):
     me = lax.axis_index("ctx")
     core = me % 2
     y = (me // 2) % 4
     x = me // 8
     first = y % 2 == 0
+    second = y % 2 == 1
+    hub = core == y % 2
+    leaf = core != y % 2
     place = me % 4
     group = y // 2
     stride = x * 2 + group
-    peer = me + 1 - 2 * core
+    chip = me - core
+    peer = chip + 1 - core
     partner = jnp.where(first, me + 2, me - 2)
-    beside = x * 8 + (jnp.where(first, y + 3, y + 1) % 4) * 2 + core
+    across = jnp.where(first, chip + 2, chip - 2) + 1 - core
+    beside = x * 8 + (jnp.where(first, y + 3, y + 1) % 4) * 2 + 1 - core
     along = [((x + d) % X) * 8 + y * 2 + core for d in range(1, X)]
 
     loads = [
@@ -69,9 +75,22 @@
         load.start()
 
     barrier = pltpu.get_barrier_semaphore()
-    for other in (peer, partner, beside, *along):
-        pl.semaphore_signal(barrier, inc=1, device_id={"ctx": other}, device_id_type=MESH)
-    pl.semaphore_wait(barrier, 6)
+
+    @pl.when(hub)
+    def _():
+        for other in (peer, partner, beside, *along):
+            pl.semaphore_signal(barrier, inc=1, device_id={"ctx": other}, device_id_type=MESH)
+
+    @pl.when(leaf)
+    def _():
+        pl.semaphore_wait(barrier, 2)
+        pl.semaphore_signal(ready.at[0], inc=1, device_id={"ctx": peer}, device_id_type=MESH)
+        pl.semaphore_signal(ready.at[1], inc=1, device_id={"ctx": partner}, device_id_type=MESH)
+
+    @pl.when(hub)
+    def _():
+        pl.semaphore_wait(ready.at[0], 1)
+        pl.semaphore_wait(ready.at[1], 1)
 
     def cols(h):
         return pl.ds(pl.multiple_of(h * HD, HD), HD)
@@ -93,32 +112,47 @@
     def vt_copy(h):
         return remote(vt.at[h], vtx.at[h], vt_s.at[h], vt_r.at[h], peer)
 
+    def out_copy(h):
+        return pltpu.make_async_copy(staged.at[h], out_hbm.at[:, cols(h)], out_sem.at[h])
+
     kx_copy = remote(k_hbm, kx, kx_s, kx_r, peer)
     gives = place != 3
     takes = place != 2
-    half_copy = remote(own_rows.at[1 - core], half_recv, st_s.at[0], st_r.at[0], peer)
-    pair_copy = remote(half, pair_recv, st_s.at[1], st_r.at[1], partner)
-    slot = table.at[core, :, pl.ds(pl.multiple_of((group * X + x) * SUMS, SUMS), SUMS), :]
+    rows_copy = remote(own_rows, rows_recv, st_s.at[0], st_r.at[0], peer)
+    pair_copy = remote(chip_rows, pair_recv, st_s.at[1], st_r.at[1], across)
+    slot_rows = pl.ds(pl.multiple_of((group * X + x) * SUMS, SUMS), SUMS)
+    slot = table.at[:, :, slot_rows, :]
     x_copies = [remote(slot, slot, x_s.at[n], x_r.at[n], to) for n, to in enumerate(along)]
-    side = table.at[core, :, pl.ds(pl.multiple_of(group * X * SUMS, X * SUMS), X * SUMS), :]
+    side = table.at[:, :, pl.ds(pl.multiple_of(group * X * SUMS, X * SUMS), X * SUMS), :]
     side_copy = remote(side, side, st_s.at[2], st_r.at[2], beside)
-    table_copy = remote(table.at[core], table.at[core], st_s.at[3], st_r.at[3], peer)
-
-    @pl.when(jnp.logical_not(first))
+    table_copy = remote(table, table, st_s.at[3], st_r.at[3], peer)
+    kf_copy = remote(k_hbm.at[:, KEPT * HD : HEADS * HD], kf.at[core], f_s.at[0], f_r.at[0], partner)
+    vf_copy = remote(vt.at[KEPT], vf.at[core], f_s.at[1], f_r.at[1], partner)
+    kf_pass = remote(kf.at[core], kf.at[core], f_s.at[2], f_r.at[2], peer)
+    vf_pass = remote(vf.at[core], vf.at[core], f_s.at[3], f_r.at[3], peer)
+
+    @pl.when(second)
     def _():
         q_copy(0).start()
 
+    @pl.when(first)
+    def _():
+        kf_copy.start()
+
     @pl.when(gives)
     def _():
         kx_copy.start()
+
+    def send_queries(h, _):
+        q_copy(h).start()
+        return 0
+
+    @pl.when(second & leaf)
+    def _():
+        lax.fori_loop(1, KEPT, send_queries, 0)
 
     loads[0].wait()
     loads[1].wait()
-
-    def stage_pair():
-        half_copy.wait_recv()
-        half[...] = own_rows[core] + half_recv[...]
-        pair_copy.start()
 
     offset = lax.broadcasted_iota(jnp.int32, (SUMS, ROWS), 1) + place * ROWS
     row = lax.broadcasted_iota(jnp.int32, (SUMS, ROWS), 0)
@@ -131,11 +165,19 @@
         picked = jnp.dot(pick, rows[...], preferred_element_type=jnp.float32).astype(jnp.bfloat16)
         for h in range(HEADS):
             own_rows[part, h] = picked[:, h * HD : (h + 1) * HD]
-    half_copy.start()
-
-    def turn(h, _):
+
+    @pl.when(leaf)
+    def _():
+        rows_copy.start()
+
+    def turn(i, _):
+        h = (i + KEPT) % HEADS
         vt[h] = v[:, cols(h)].T
 
+        @pl.when(first & (i == 0))
+        def _():
+            vf_copy.start()
+
         @pl.when(gives)
         def _():
             vt_copy(h).start()
@@ -143,15 +185,16 @@
         return 0
 
     lax.fori_loop(0, HEADS, turn, 0)
-    stage_pair()
-
-    @pl.when(jnp.logical_not(first))
-    def _():
-        def send(h, _):
-            q_copy(h).start()
-            return 0
-
-        lax.fori_loop(1, HEADS, send, 0)
+
+    @pl.when(hub)
+    def _():
+        rows_copy.wait_recv()
+        chip_rows[...] = own_rows[...] + rows_recv[...]
+        pair_copy.start()
+
+    @pl.when(second & hub)
+    def _():
+        lax.fori_loop(1, KEPT, send_queries, 0)
 
     loads[2].wait()
 
@@ -173,39 +216,34 @@
         def _():
             keep([(k[:, cols(h)], vt[h], key_id <= query_id), (kx[:, cols(h)], vtx[h], None)])
 
-    def finish(h, remote_part):
+    def fold(h, total, top, weight):
+        high = jnp.maximum(acc_max[h], top)
+        scale_old = jnp.exp2(acc_max[h] - high)
+        scale_new = jnp.exp2(top - high)
+        return acc[h] * scale_old + total * scale_new, high, acc_sum[h] * scale_old + weight * scale_new
+
+    def fold_summary(h):
         seen = lax.broadcasted_iota(jnp.int32, (STRIDES * SUMS, ROWS), 0) // SUMS
         seen = (seen % X) * 2 + seen // X < stride
-        total, top, weight = attend([(table[0, h], table[1, h].T, seen)], q[:, cols(h)])
-        high = jnp.maximum(top, acc_max[h])
-        if remote_part:
-            high = jnp.maximum(high, lse_recv[h])
-        scale_sum = jnp.exp2(top - high)
-        scale_own = jnp.exp2(acc_max[h] - high)
-        top_part = total * scale_sum + acc[h] * scale_own
-        low_part = weight * scale_sum + acc_sum[h] * scale_own
-        if remote_part:
-            scale_far = jnp.exp2(lse_recv[h] - high)
-            top_part = top_part + o_recv[h].astype(jnp.float32) * scale_far
-            low_part = low_part + scale_far
-        staged[h] = (top_part / low_part).astype(jnp.bfloat16).T
+        return fold(h, *attend([(table[0, h], table[1, h].T, seen)], q[:, cols(h)]))
+
+    def put_out(h, total, weight):
+        staged[h] = (total / weight).astype(jnp.bfloat16).T
         out_copy(h).start()
 
-    def out_copy(h):
-        return pltpu.make_async_copy(staged.at[h], out_hbm.at[:, cols(h)], out_sem.at[h])
-
-    def stage_x():
+    def to_x():
         pair_copy.wait_recv()
-        table[core, :, pl.ds(pl.multiple_of((group * X + x) * SUMS, SUMS), SUMS), :] = half[...] + pair_recv[...]
+        table[:, :, slot_rows, :] = chip_rows[...] + pair_recv[...]
+        pl.semaphore_wait(barrier, 4)
         for copy in x_copies:
             copy.start()
 
-    def stage_side():
+    def to_side():
         for copy in x_copies:
             copy.wait_recv()
         side_copy.start()
 
-    def stage_table():
+    def to_peer():
         side_copy.wait_recv()
         table_copy.start()
 
@@ -218,10 +256,7 @@
         def _():
             vt_copy(h).wait_recv()
 
-        local(h)
-        pl.when(h == 1)(stage_side)
-
-        @pl.when(first)
+        @pl.when(first & (h < KEPT))
         def _():
             q_copy(h).wait_recv()
             total, top, weight = attend(
@@ -229,34 +264,67 @@
             )
             o_send[h] = (total / weight).astype(jnp.bfloat16)
             lse_send[h] = top + jnp.log2(weight)
+            lse_copy(h).start()
             o_copy(h).start()
-            lse_copy(h).start()
-
-        pl.when(h == 0)(stage_x)
-        pl.when(h == 1)(stage_table)
-
-        @pl.when(h == 3)
-        def _():
-            table_copy.wait_recv()
-
-        @pl.when(first & (h >= 4))
-        def _():
-            finish(2 * (h - 4), False)
-            finish(2 * (h - 4) + 1, False)
+
+        local(h)
+        pl.when(hub & (h == jnp.where(first, 0, 2)))(to_x)
+        pl.when(hub & (h == jnp.where(first, 2, 6)))(to_side)
+        pl.when(hub & first & (h == 4))(to_peer)
+
+        @pl.when(second & (h == 3))
+        def _():
+            kf_copy.wait_recv()
+            vf_copy.wait_recv()
+            kf_pass.start()
+            vf_pass.start()
 
         return 0
 
     lax.fori_loop(0, HEADS, step, 0)
-
-    @pl.when(jnp.logical_not(first))
-    def _():
-        def merge(h, _):
+    pl.when(hub & second)(to_peer)
+
+    @pl.when(second)
+    def _():
+        kf_pass.wait_recv()
+        vf_pass.wait_recv()
+        total, top, weight = fold(
+            KEPT, *attend([(kf[0], vf[0], None), (kf[1], vf[1], None)], q[:, KEPT * HD : HEADS * HD])
+        )
+        acc[KEPT] = total
+        acc_max[KEPT] = top
+        acc_sum[KEPT] = weight
+
+    @pl.when(leaf)
+    def _():
+        table_copy.wait_recv()
+
+    @pl.when(first)
+    def _():
+        def close(h, _):
+            total, _, weight = fold_summary(h)
+            put_out(h, total, weight)
+            return 0
+
+        lax.fori_loop(0, HEADS, close, 0)
+
+    @pl.when(second)
+    def _():
+        total, _, weight = fold_summary(KEPT)
+        put_out(KEPT, total, weight)
+
+        def close(h, _):
+            total, top, weight = fold_summary(h)
+            acc[h] = total
+            lse_copy(h).wait_recv()
             o_copy(h).wait_recv()
-            lse_copy(h).wait_recv()
-            finish(h, True)
+            high = jnp.maximum(top, lse_recv[h])
+            near = jnp.exp2(top - high)
+            far = jnp.exp2(lse_recv[h] - high)
+            put_out(h, acc[h] * near + o_recv[h].astype(jnp.float32) * far, weight * near + far)
             return 0
 
-        lax.fori_loop(0, HEADS, merge, 0)
+        lax.fori_loop(0, KEPT, close, 0)
 
     def drain(h, _):
         out_copy(h).wait()
@@ -265,12 +333,12 @@
         def _():
             vt_copy(h).wait_send()
 
-        @pl.when(first)
+        @pl.when(first & (h < KEPT))
         def _():
             o_copy(h).wait_send()
             lse_copy(h).wait_send()
 
-        @pl.when(jnp.logical_not(first))
+        @pl.when(second & (h < KEPT))
         def _():
             q_copy(h).wait_send()
 
@@ -282,8 +350,24 @@
     def _():
         kx_copy.wait_send()
 
-    for copy in (half_copy, pair_copy, *x_copies, side_copy, table_copy):
-        copy.wait_send()
+    @pl.when(first)
+    def _():
+        kf_copy.wait_send()
+        vf_copy.wait_send()
+
+    @pl.when(second)
+    def _():
+        kf_pass.wait_send()
+        vf_pass.wait_send()
+
+    @pl.when(leaf)
+    def _():
+        rows_copy.wait_send()
+
+    @pl.when(hub)
+    def _():
+        for copy in (pair_copy, *x_copies, side_copy, table_copy):
+            copy.wait_send()
 
 
 def on_device(query_rows, key_rows, value_rows, summary_pos):
@@ -313,10 +397,12 @@
             pltpu.VMEM((HEADS, 1, ROWS), f32),
             pltpu.VMEM((HEADS, ROWS, HD), bf16),
             pltpu.VMEM((2, HEADS, SUMS, HD), bf16),
-            pltpu.VMEM((HEADS, SUMS, HD), bf16),
-            pltpu.VMEM((HEADS, SUMS, HD), bf16),
-            pltpu.VMEM((HEADS, SUMS, HD), bf16),
+            pltpu.VMEM((2, HEADS, SUMS, HD), bf16),
+            pltpu.VMEM((2, HEADS, SUMS, HD), bf16),
+            pltpu.VMEM((2, HEADS, SUMS, HD), bf16),
             pltpu.VMEM((2, HEADS, STRIDES * SUMS, HD), bf16),
+            pltpu.VMEM((2, ROWS, HD), bf16),
+            pltpu.VMEM((2, HD, ROWS), bf16),
             dma((3,)),
             per_head, per_head,
             dma, dma,
@@ -326,6 +412,8 @@
             per_head,
             dma((4,)), dma((4,)),
             dma((X - 1,)), dma((X - 1,)),
+            dma((4,)), dma((4,)),
+            pltpu.SemaphoreType.REGULAR((2,)),
         ],
         compiler_params=pltpu.CompilerParams(
             collective_id=0, has_side_effects=True, vmem_limit_bytes=52 * 2**20

time: 40.1 us -> 36.8 us (0.918)
  the two profiles are of different devices: /device:TPU:206 before, /device:TPU:1 now
where the time goes in v3:
time: 36.8 us; the launch traced here: 36.7 us
  Pallas kernels  35.7 us (97%)
  local copies, waits for them, and re-layouts  0.97 us (3%)
    pallas_call x1, Pallas kernels, on_device(): pl.pallas_call(kernel, out_shape=jax.ShapeDtypeStruct(query_rows.shape, b...  35.7 us
    unnamed x1, local copies, waits for them, and re-layouts  0.97 us

profile of v3, /device:TPU:1, one launch (start us, length us, event | category | flops | bytes accessed | tf_op | source)
XLA Modules:
  0.0 36.7 jit_solution(9578728228539848077)
XLA Ops:
  0.0 35.7 %shard_map.46 = bf16[512,1024]{1,0:T(8,128)(2,1)S(1)} custom-call(bf16[512,1024]{1,0:T(8,128)(2,1)} %q_hbm.1, bf16[512,1024]{1,0:T(8,128)(2,1)} %k_hbm.1, bf16[512,1024]{1,0:T(8,128)(2,1)} %v_hbm.1, s32[8,16]{1,0:T(8,128)} %pos_ref.1), custom_call_target="tpu_custom_call" | custom-call | tf_op jit(solution)/shard_map/pallas_call | solution.py:378
  35.7 1.0 %copy.6 = bf16[512,1024]{1,0:T(8,128)(2,1)} copy(bf16[512,1024]{1,0:T(8,128)(2,1)S(1)} %shard_map.46) | data formatting | bytes 2097152

commit v4 on v3

--- a/solution.py
+++ b/solution.py
@@ -1,5 +1,3 @@
-import functools
-
 import jax
 import jax.numpy as jnp
 import numpy as np
@@ -26,21 +24,38 @@
     )
 
 
-def attend(parts, queries):
-    raw = []
-    for keys, _, mask in parts:
-        s = scores(keys, queries)
-        raw.append(s if mask is None else jnp.where(mask, s, FLOOR))
-    top = functools.reduce(jnp.maximum, [jnp.max(s, axis=0, keepdims=True) for s in raw]) * RATE
-    total = None
-    weight = None
-    for s, (_, values, _) in zip(raw, parts):
-        p = jnp.exp2(s * RATE - top)
-        part_weight = jnp.sum(p, axis=0, keepdims=True)
-        part = jnp.dot(values, p.astype(jnp.bfloat16), preferred_element_type=jnp.float32)
-        total = part if total is None else total + part
-        weight = part_weight if weight is None else weight + part_weight
-    return total, top, weight
+def weigh(s):
+    top = jnp.max(s, axis=0, keepdims=True) * RATE
+    p = jnp.exp2(s * RATE - top)
+    return p.astype(jnp.bfloat16), top, jnp.sum(p, axis=0, keepdims=True)
+
+
+def mix(values, p):
+    return jnp.dot(values, p, preferred_element_type=jnp.float32)
+
+
+def attend(keys, values, queries, mask=None):
+    s = scores(keys, queries)
+    p, top, weight = weigh(s if mask is None else jnp.where(mask, s, FLOOR))
+    return mix(values, p), top, weight
+
+
+def attend_causal(keys, values, queries):
+    half = ROWS // 2
+    seen = lax.broadcasted_iota(jnp.int32, (half, half), 0) <= lax.broadcasted_iota(jnp.int32, (half, half), 1)
+    early = scores(keys[:half], queries)
+    late = jnp.where(seen, scores(keys[half:], queries[half:]), FLOOR)
+    p, top, weight = weigh(jnp.where(seen, early[:, :half], FLOOR))
+    low = mix(values[:, :half], p)
+    p2, top2, weight2 = weigh(jnp.concatenate([early[:, half:], late], axis=0))
+    high = mix(values, p2)
+    return tuple(jnp.concatenate(pair, axis=1) for pair in ((low, high), (top, top2), (weight, weight2)))
+
+
+def join(one, two):
+    top = jnp.maximum(one[1], two[1])
+    a, b = jnp.exp2(one[1] - top), jnp.exp2(two[1] - top)
+    return one[0] * a + two[0] * b, top, one[2] * a + two[2] * b
 
 
 def kernel(
@@ -83,14 +98,13 @@
 
     @pl.when(leaf)
     def _():
-        pl.semaphore_wait(barrier, 2)
-        pl.semaphore_signal(ready.at[0], inc=1, device_id={"ctx": peer}, device_id_type=MESH)
-        pl.semaphore_signal(ready.at[1], inc=1, device_id={"ctx": partner}, device_id_type=MESH)
+        pl.semaphore_signal(barrier, inc=1, device_id={"ctx": across}, device_id_type=MESH)
+        pl.semaphore_wait(barrier, 3)
+        pl.semaphore_signal(ready, inc=1, device_id={"ctx": peer}, device_id_type=MESH)
 
     @pl.when(hub)
     def _():
-        pl.semaphore_wait(ready.at[0], 1)
-        pl.semaphore_wait(ready.at[1], 1)
+        pl.semaphore_wait(ready, 1)
 
     def cols(h):
         return pl.ds(pl.multiple_of(h * HD, HD), HD)
@@ -198,37 +212,26 @@
 
     loads[2].wait()
 
-    key_id = lax.broadcasted_iota(jnp.int32, (ROWS, ROWS), 0)
-    query_id = lax.broadcasted_iota(jnp.int32, (ROWS, ROWS), 1)
-
     def local(h):
-        def keep(parts):
-            total, top, weight = attend(parts, q[:, cols(h)])
-            acc[h] = total
-            acc_max[h] = top
-            acc_sum[h] = weight
-
-        @pl.when(core == 0)
-        def _():
-            keep([(k[:, cols(h)], vt[h], key_id <= query_id)])
-
-        @pl.when(core == 1)
-        def _():
-            keep([(k[:, cols(h)], vt[h], key_id <= query_id), (kx[:, cols(h)], vtx[h], None)])
-
-    def fold(h, total, top, weight):
-        high = jnp.maximum(acc_max[h], top)
-        scale_old = jnp.exp2(acc_max[h] - high)
-        scale_new = jnp.exp2(top - high)
-        return acc[h] * scale_old + total * scale_new, high, acc_sum[h] * scale_old + weight * scale_new
-
-    def fold_summary(h):
-        seen = lax.broadcasted_iota(jnp.int32, (STRIDES * SUMS, ROWS), 0) // SUMS
-        seen = (seen % X) * 2 + seen // X < stride
-        return fold(h, *attend([(table[0, h], table[1, h].T, seen)], q[:, cols(h)]))
+        return attend_causal(k[:, cols(h)], vt[h], q[:, cols(h)])
+
+    def before(h):
+        return attend(kx[:, cols(h)], vtx[h], q[:, cols(h)])
+
+    def keep(h, part):
+        acc[h], acc_max[h], acc_sum[h] = part
+
+    def kept(h):
+        return acc[h], acc_max[h], acc_sum[h]
+
+    column = lax.broadcasted_iota(jnp.int32, (STRIDES * SUMS, 1), 0) // SUMS
+    seen = (column % X) * 2 + column // X < stride
+
+    def with_summary(h):
+        return join(kept(h), attend(table[0, h], table[1, h].T, q[:, cols(h)], seen))
 
     def put_out(h, total, weight):
-        staged[h] = (total / weight).astype(jnp.bfloat16).T
+        staged[h] = (total * (1.0 / weight)).astype(jnp.bfloat16).T
         out_copy(h).start()
 
     def to_x():
@@ -247,84 +250,133 @@
         side_copy.wait_recv()
         table_copy.start()
 
-    def step(h, _):
-        @pl.when((h == 0) & takes)
+    def wait_peer(h):
+        @pl.when(h == 0)
         def _():
             kx_copy.wait_recv()
 
-        @pl.when(takes)
-        def _():
-            vt_copy(h).wait_recv()
-
-        @pl.when(first & (h < KEPT))
-        def _():
+        vt_copy(h).wait_recv()
+
+    def serve(h):
+        queries = qr[h]
+        total, top, weight = join(
+            attend(k[:, cols(h)], vt[h], queries), attend(kx[:, cols(h)], vtx[h], queries)
+        )
+        o_send[h] = (total * (1.0 / weight)).astype(jnp.bfloat16)
+        lse_send[h] = top + jnp.log2(weight)
+
+    def reply(h):
+        lse_copy(h).start()
+        o_copy(h).start()
+
+    def close(h):
+        total, _, weight = with_summary(h)
+        put_out(h, total, weight)
+
+    @pl.when(first & hub)
+    def _():
+        def step(h, _):
+            wait_peer(h)
+            keep(h, local(h))
+
+            @pl.when(h == 5)
+            def _():
+                to_peer()
+
             q_copy(h).wait_recv()
-            total, top, weight = attend(
-                [(k[:, cols(h)], vt[h], None), (kx[:, cols(h)], vtx[h], None)], qr[h]
-            )
-            o_send[h] = (total / weight).astype(jnp.bfloat16)
-            lse_send[h] = top + jnp.log2(weight)
-            lse_copy(h).start()
-            o_copy(h).start()
-
-        local(h)
-        pl.when(hub & (h == jnp.where(first, 0, 2)))(to_x)
-        pl.when(hub & (h == jnp.where(first, 2, 6)))(to_side)
-        pl.when(hub & first & (h == 4))(to_peer)
-
-        @pl.when(second & (h == 3))
+            serve(h)
+            reply(h)
+            pl.when(h == 1)(to_x)
+            pl.when(h == 3)(to_side)
+            return 0
+
+        lax.fori_loop(0, KEPT, step, 0)
+        wait_peer(KEPT)
+        keep(KEPT, local(KEPT))
+
+    @pl.when(first & leaf)
+    def _():
+        def step(h, _):
+            wait_peer(h)
+            keep(h, join(local(h), before(h)))
+
+            q_copy(h).wait_recv()
+            serve(h)
+            reply(h)
+            return 0
+
+        lax.fori_loop(0, KEPT, step, 0)
+        wait_peer(KEPT)
+        keep(KEPT, join(local(KEPT), before(KEPT)))
+        table_copy.wait_recv()
+
+    def pass_on(i):
+        @pl.when(i == 1)
         def _():
             kf_copy.wait_recv()
             vf_copy.wait_recv()
             kf_pass.start()
             vf_pass.start()
 
-        return 0
-
-    lax.fori_loop(0, HEADS, step, 0)
-    pl.when(hub & second)(to_peer)
+    @pl.when(second & leaf)
+    def _():
+        def step(i, _):
+            h = 2 * i
+            keep(h, local(h))
+            keep(h + 1, local(h + 1))
+            pass_on(i)
+            return 0
+
+        lax.fori_loop(0, HEADS // 2, step, 0)
+
+    @pl.when(second & hub)
+    def _():
+        def step(i, _):
+            h = 2 * i
+            wait_peer(h)
+            vt_copy(h + 1).wait_recv()
+            keep(h, join(local(h), before(h)))
+            keep(h + 1, join(local(h + 1), before(h + 1)))
+            pl.when(i == 1)(to_x)
+            pass_on(i)
+            pl.when(i == 3)(to_side)
+            return 0
+
+        lax.fori_loop(0, HEADS // 2, step, 0)
+
+    @pl.when(first)
+    def _():
+        def closes(i, _):
+            close(2 * i)
+            close(2 * i + 1)
+            return 0
+
+        lax.fori_loop(0, HEADS // 2, closes, 0)
 
     @pl.when(second)
     def _():
         kf_pass.wait_recv()
         vf_pass.wait_recv()
-        total, top, weight = fold(
-            KEPT, *attend([(kf[0], vf[0], None), (kf[1], vf[1], None)], q[:, KEPT * HD : HEADS * HD])
-        )
-        acc[KEPT] = total
-        acc_max[KEPT] = top
-        acc_sum[KEPT] = weight
-
-    @pl.when(leaf)
-    def _():
-        table_copy.wait_recv()
-
-    @pl.when(first)
-    def _():
-        def close(h, _):
-            total, _, weight = fold_summary(h)
-            put_out(h, total, weight)
-            return 0
-
-        lax.fori_loop(0, HEADS, close, 0)
-
-    @pl.when(second)
-    def _():
-        total, _, weight = fold_summary(KEPT)
-        put_out(KEPT, total, weight)
-
-        def close(h, _):
-            total, top, weight = fold_summary(h)
-            acc[h] = total
+        queries = q[:, KEPT * HD : HEADS * HD]
+        far = join(attend(kf[0], vf[0], queries), attend(kf[1], vf[1], queries))
+        keep(KEPT, join(kept(KEPT), far))
+        pl.when(hub)(to_peer)
+
+        @pl.when(leaf)
+        def _():
+            table_copy.wait_recv()
+
+        close(KEPT)
+
+        def finish(h, _):
+            keep(h, with_summary(h))
             lse_copy(h).wait_recv()
             o_copy(h).wait_recv()
-            high = jnp.maximum(top, lse_recv[h])
-            near = jnp.exp2(top - high)
-            far = jnp.exp2(lse_recv[h] - high)
-            put_out(h, acc[h] * near + o_recv[h].astype(jnp.float32) * far, weight * near + far)
-            return 0
-
-        lax.fori_loop(0, KEPT, close, 0)
+            total, _, weight = join(kept(h), (o_recv[h].astype(jnp.float32), lse_recv[h], 1.0))
+            put_out(h, total, weight)
+            return 0
+
+        lax.fori_loop(0, KEPT, finish, 0)
 
     def drain(h, _):
         out_copy(h).wait()
@@ -413,7 +465,7 @@
             dma((4,)), dma((4,)),
             dma((X - 1,)), dma((X - 1,)),
             dma((4,)), dma((4,)),
-            pltpu.SemaphoreType.REGULAR((2,)),
+            pltpu.SemaphoreType.REGULAR,
         ],
         compiler_params=pltpu.CompilerParams(
             collective_id=0, has_side_effects=True, vmem_limit_bytes=52 * 2**20

time: 36.8 us -> 36 us (0.978)
  Pallas kernels: 35.7 us -> 34.9 us
    pallas_call x1, Pallas kernels: 35.7 us -> 34.9 us  [on_device(): pl.pallas_call(kernel, out_shape=jax.ShapeDtypeStruct(query_rows.shape, b...]
where the time goes in v4:
time: 36 us; the launch traced here: 35.9 us
  Pallas kernels  34.9 us (97%)
  local copies, waits for them, and re-layouts  0.97 us (3%)
    pallas_call x1, Pallas kernels, on_device(): pl.pallas_call(kernel, out_shape=jax.ShapeDtypeStruct(query_rows.shape, b...  34.9 us
    unnamed x1, local copies, waits for them, and re-layouts  0.97 us

profile of v4, /device:TPU:1, one launch (start us, length us, event | category | flops | bytes accessed | tf_op | source)
XLA Modules:
  0.0 35.9 jit_solution(17387721151792360239)
XLA Ops:
  0.0 34.9 %shard_map.46 = bf16[512,1024]{1,0:T(8,128)(2,1)S(1)} custom-call(bf16[512,1024]{1,0:T(8,128)(2,1)} %q_hbm.1, bf16[512,1024]{1,0:T(8,128)(2,1)} %k_hbm.1, bf16[512,1024]{1,0:T(8,128)(2,1)} %v_hbm.1, s32[8,16]{1,0:T(8,128)} %pos_ref.1), custom_call_target="tpu_custom_call" | custom-call | tf_op jit(solution)/shard_map/pallas_call | solution.py:430
  35.0 1.0 %copy.6 = bf16[512,1024]{1,0:T(8,128)(2,1)} copy(bf16[512,1024]{1,0:T(8,128)(2,1)S(1)} %shard_map.46) | data formatting | bytes 2097152

commit v5 on v4

--- a/solution.py
+++ b/solution.py
@@ -82,19 +82,19 @@
     beside = x * 8 + (jnp.where(first, y + 3, y + 1) % 4) * 2 + 1 - core
     along = [((x + d) % X) * 8 + y * 2 + core for d in range(1, X)]
 
+    barrier = pltpu.get_barrier_semaphore()
+
+    @pl.when(hub)
+    def _():
+        for other in (peer, partner, beside, *along):
+            pl.semaphore_signal(barrier, inc=1, device_id={"ctx": other}, device_id_type=MESH)
+
     loads = [
         pltpu.make_async_copy(src, dst, load_sem.at[n])
         for n, (src, dst) in enumerate(((k_hbm, k), (v_hbm, v), (q_hbm, q)))
     ]
     for load in loads:
         load.start()
-
-    barrier = pltpu.get_barrier_semaphore()
-
-    @pl.when(hub)
-    def _():
-        for other in (peer, partner, beside, *along):
-            pl.semaphore_signal(barrier, inc=1, device_id={"ctx": other}, device_id_type=MESH)
 
     @pl.when(leaf)
     def _():
@@ -279,6 +279,11 @@
             wait_peer(h)
             keep(h, local(h))
 
+            @pl.when(h == 3)
+            def _():
+                vt_copy(KEPT).wait_recv()
+                keep(KEPT, local(KEPT))
+
             @pl.when(h == 5)
             def _():
                 to_peer()
@@ -291,12 +296,15 @@
             return 0
 
         lax.fori_loop(0, KEPT, step, 0)
-        wait_peer(KEPT)
-        keep(KEPT, local(KEPT))
 
     @pl.when(first & leaf)
     def _():
         def step(h, _):
+            @pl.when(h == 4)
+            def _():
+                vt_copy(KEPT).wait_recv()
+                keep(KEPT, join(local(KEPT), before(KEPT)))
+
             wait_peer(h)
             keep(h, join(local(h), before(h)))
 
@@ -306,8 +314,6 @@
             return 0
 
         lax.fori_loop(0, KEPT, step, 0)
-        wait_peer(KEPT)
-        keep(KEPT, join(local(KEPT), before(KEPT)))
         table_copy.wait_recv()
 
     def pass_on(i):
@@ -347,11 +353,11 @@
     @pl.when(first)
     def _():
         def closes(i, _):
-            close(2 * i)
-            close(2 * i + 1)
-            return 0
-
-        lax.fori_loop(0, HEADS // 2, closes, 0)
+            for n in range(4):
+                close(4 * i + n)
+            return 0
+
+        lax.fori_loop(0, HEADS // 4, closes, 0)
 
     @pl.when(second)
     def _():

time: 36 us -> 35.1 us (0.975)
  Pallas kernels: 34.9 us -> 34 us
    pallas_call x1, Pallas kernels: 34.9 us -> 34 us  [on_device(): pl.pallas_call(kernel, out_shape=jax.ShapeDtypeStruct(query_rows.shape, b...]
where the time goes in v5:
time: 35.1 us; the launch traced here: 34.9 us
  Pallas kernels  34 us (97%)
  local copies, waits for them, and re-layouts  0.97 us (3%)
    pallas_call x1, Pallas kernels, on_device(): pl.pallas_call(kernel, out_shape=jax.ShapeDtypeStruct(query_rows.shape, b...  34 us
    unnamed x1, local copies, waits for them, and re-layouts  0.97 us

profile of v5, /device:TPU:1, one launch (start us, length us, event | category | flops | bytes accessed | tf_op | source)
XLA Modules:
  0.0 34.9 jit_solution(18284206218220592661)
XLA Ops:
  0.0 34.0 %shard_map.46 = bf16[512,1024]{1,0:T(8,128)(2,1)S(1)} custom-call(bf16[512,1024]{1,0:T(8,128)(2,1)} %q_hbm.1, bf16[512,1024]{1,0:T(8,128)(2,1)} %k_hbm.1, bf16[512,1024]{1,0:T(8,128)(2,1)} %v_hbm.1, s32[8,16]{1,0:T(8,128)} %pos_ref.1), custom_call_target="tpu_custom_call" | custom-call | tf_op jit(solution)/shard_map/pallas_call | solution.py:436
  34.0 1.0 %copy.6 = bf16[512,1024]{1,0:T(8,128)(2,1)} copy(bf16[512,1024]{1,0:T(8,128)(2,1)S(1)} %shard_map.46) | data formatting | bytes 2097152

commit v6 on v5

--- a/solution.py
+++ b/solution.py
@@ -259,9 +259,11 @@
 
     def serve(h):
         queries = qr[h]
-        total, top, weight = join(
-            attend(k[:, cols(h)], vt[h], queries), attend(kx[:, cols(h)], vtx[h], queries)
-        )
+        near, far = scores(k[:, cols(h)], queries), scores(kx[:, cols(h)], queries)
+        top = jnp.maximum(jnp.max(near, axis=0, keepdims=True), jnp.max(far, axis=0, keepdims=True)) * RATE
+        p, p2 = jnp.exp2(near * RATE - top), jnp.exp2(far * RATE - top)
+        weight = jnp.sum(p, axis=0, keepdims=True) + jnp.sum(p2, axis=0, keepdims=True)
+        total = mix(vt[h], p.astype(jnp.bfloat16)) + mix(vtx[h], p2.astype(jnp.bfloat16))
         o_send[h] = (total * (1.0 / weight)).astype(jnp.bfloat16)
         lse_send[h] = top + jnp.log2(weight)
 

time: 35.1 us -> 34.7 us (0.989)
  Pallas kernels: 34 us -> 33.6 us
where the time goes in v6:
time: 34.7 us; the launch traced here: 34.6 us
  Pallas kernels  33.6 us (97%)
  local copies, waits for them, and re-layouts  0.97 us (3%)
    pallas_call x1, Pallas kernels, on_device(): pl.pallas_call(kernel, out_shape=jax.ShapeDtypeStruct(query_rows.shape, b...  33.6 us
    unnamed x1, local copies, waits for them, and re-layouts  0.97 us

profile of v6, /device:TPU:1, one launch (start us, length us, event | category | flops | bytes accessed | tf_op | source)
XLA Modules:
  0.0 34.6 jit_solution(11594903503580390062)
XLA Ops:
  0.0 33.6 %shard_map.46 = bf16[512,1024]{1,0:T(8,128)(2,1)S(1)} custom-call(bf16[512,1024]{1,0:T(8,128)(2,1)} %q_hbm.1, bf16[512,1024]{1,0:T(8,128)(2,1)} %k_hbm.1, bf16[512,1024]{1,0:T(8,128)(2,1)} %v_hbm.1, s32[8,16]{1,0:T(8,128)} %pos_ref.1), custom_call_target="tpu_custom_call" | custom-call | tf_op jit(solution)/shard_map/pallas_call | solution.py:438
  33.6 1.0 %copy.6 = bf16[512,1024]{1,0:T(8,128)(2,1)} copy(bf16[512,1024]{1,0:T(8,128)(2,1)S(1)} %shard_map.46) | data formatting | bytes 2097152
